TPU v7x, 128 devices: a whole 4x4x4 slice. The times are simulated.
128 devices in a mesh: sec: 2 (over core), dev: 64 (over y, x, z).
Axes of the slice: x: 4, y: 4, z: 4, core: 2. Of those that a mesh axis runs over, the one named last changes fastest.
Arguments:
- queries: bfloat16 [512, 128, 576], P('dev', 'sec'), may hold values from -11 to 11
- cache: bfloat16 [512, 256, 576], P('dev'), may hold values from -2.2 to 2.2
- lengths: int32 [512], P('dev'), may hold values from 1 to 256, 65536 in all
- hidden_rows: bfloat16 [1024, 7168], P(('sec', 'dev')), may hold values from -6 to 6
- routes: int32 [1024, 8], P(('sec', 'dev')), may hold values from 0 to 31, all different within a row; in each aligned block of 8 rows (0 to 7, 8 to 15, ...) at most 3 rows name the same one
- gate_codes: int32 [1024, 8], P(('sec', 'dev')), may hold values from 1 to 65535
- placement: int32 [32], replicated, may hold values from 0 to 31, each once
- w_gate_up: bfloat16 [2, 7168, 65536], P(None, None, ('sec', 'dev')), may hold values from -0.0625 to 0.0625
- w_down: bfloat16 [65536, 7168], P(('sec', 'dev')), may hold values from -0.125 to 0.125
Outputs:
- context: bfloat16 [512, 128, 512], P('dev', 'sec')
- mixed: bfloat16 [1024, 7168], P(('sec', 'dev'))
Inputs may be any that keep to these rules, and one draw needn't show every extreme that they name: `routes`: each row names 8 different experts; in the tokens of one device no expert is named by more than 3 tokens, a bound that some block reaches.
All inputs are finite; a program needn't handle non-finite values. No bound on the sum of `lengths` on one device may be relied on, other than what follows from the above.
Results may differ from a plain program's by a relative error of at most 0.0057.
Values may be sent and summed in bfloat16 or wider, within the bound.
No kernel may reach another device: no remote copies, remote signals or barrier semaphores. Data moves between devices by JAX's collectives and lax.ppermute only.
A program may use at most 128 MiB of HBM per device.

v0:
```python
import jax
import jax.numpy as jnp
from jax import lax
from jax.experimental import pallas as pl
from jax.sharding import PartitionSpec as P

D = 7168
LATENT = 512
EXPERTS = 32
CAP = 3
ROWS = 8
TOPK = 8
SCORE_SCALE = 192.0 ** (-0.5)

AXES = ("sec", "dev")
GRAY = (0, 1, 3, 2)
FIRST = ((1, 2, 32), (4, 8, 16))
SECOND = ((8, 16, 4), (2, 32, 1))
CUBE = 8
TABLE = 128
SLOT_ROWS = 24
EDGES = (0, 2560, 7168)
OUT_EDGES = (0, 2304, 4736, 7168)


def code_of(dev):
    y, x, z = dev // 16, (dev // 4) % 4, dev % 4
    return GRAY[z] | GRAY[x] << 2 | GRAY[y] << 4


def dev_of(code):
    return GRAY[code & 3] | GRAY[(code >> 2) & 3] << 2 | GRAY[(code >> 4) & 3] << 4


def masks_of(bits):
    return [sum(bit for i, bit in enumerate(bits) if k >> i & 1) for k in range(CUBE)]


def cube_exchange(rows, cube):
    groups = []
    for sec in range(2):
        masks = masks_of(cube[sec])
        for base in range(64):
            if base & masks[-1] == 0:
                groups.append([sec * 64 + dev_of(base | mask) for mask in masks])
    return lax.all_to_all(rows, AXES, 0, 0, tiled=True, axis_index_groups=groups)


def swap_cores(rows):
    return lax.ppermute(rows, "sec", [(0, 1), (1, 0)])


def attend(queries, cache, lengths):
    scores = (
        jnp.einsum("rhc,rlc->rhl", queries, cache, preferred_element_type=jnp.float32) * SCORE_SCALE
    )
    places = lax.broadcasted_iota(jnp.int32, scores.shape, 2)
    scores = jnp.where(places < lengths[:, None, None], scores, -1e30)
    peak_score = jnp.max(scores, axis=2, keepdims=True)
    raised = jnp.exp(scores - peak_score)
    weights = (raised / jnp.sum(raised, axis=2, keepdims=True)).astype(jnp.bfloat16)
    return jnp.einsum(
        "rhl,rlc->rhc", weights, cache[:, :, :LATENT], preferred_element_type=jnp.float32
    ).astype(jnp.bfloat16)


def outgoing_kernel(hidden_ref, routes_ref, codes_ref, out_ref):
    codes = codes_ref[...].astype(jnp.float32)
    gates = 2.5 * codes / jnp.sum(codes, axis=1, keepdims=True)
    routes = routes_ref[...]
    lanes = lax.broadcasted_iota(jnp.int32, (ROWS, TABLE), 1)
    member = jnp.zeros((ROWS, TABLE), jnp.float32)
    table = jnp.zeros((ROWS, TABLE), jnp.float32)
    for k in range(TOPK):
        expert = routes[:, k : k + 1]
        member = jnp.where(lanes == expert, 1.0, member)
        table = jnp.where(lanes == expert + EXPERTS, gates[:, k : k + 1], table)
    rank = member
    for back in range(1, ROWS):
        rank = rank + jnp.concatenate(
            [jnp.zeros((back, TABLE), jnp.float32), member[: ROWS - back]], axis=0
        )
    table = (table + rank * member).astype(jnp.bfloat16)
    row = jnp.concatenate([hidden_ref[...], table], axis=1)
    out_ref[...] = jnp.concatenate([row] * CUBE, axis=0)


def outgoing_rows(hidden_rows, routes, gate_codes):
    return pl.pallas_call(
        outgoing_kernel,
        out_shape=jax.ShapeDtypeStruct((CUBE * ROWS, D + TABLE), jnp.bfloat16),
    )(hidden_rows, routes, gate_codes)


def columns_of_cube():
    sec, dev = lax.axis_index("sec"), lax.axis_index("dev")

    def gray(place):
        return place ^ (place >> 1)

    code = gray(dev % 4) | gray(dev // 4 % 4) << 2 | gray(dev // 16) << 4
    masks = jnp.where(
        sec == 0, jnp.asarray(masks_of(SECOND[0])), jnp.asarray(masks_of(SECOND[1]))
    ).astype(jnp.int32)
    codes = (code & ~masks[-1]) | masks
    return gray(codes >> 4) * 4 + gray((codes >> 2) & 3)


def picks_of(tables, experts):
    count, tokens = experts.shape[0], tables.shape[0]
    picks = experts[None, :] + EXPERTS * jnp.arange(2)[:, None]
    onehot = (lax.broadcasted_iota(jnp.int32, (2, count, TABLE), 2) == picks[:, :, None]).astype(
        jnp.bfloat16
    )
    fields = jnp.einsum("fsc,tc->fst", onehot, tables, preferred_element_type=jnp.float32)
    shape = (count, SLOT_ROWS, tokens)
    row_ids = lax.broadcasted_iota(jnp.int32, shape, 1)
    token_ids = lax.broadcasted_iota(jnp.int32, shape, 2)
    chosen = (row_ids // CAP == token_ids // ROWS) & (
        fields[0][:, None, :] == (row_ids % CAP + 1).astype(jnp.float32)
    )
    weighted = jnp.where(chosen, fields[1][:, None, :], 0.0)
    return tuple(
        a.astype(jnp.bfloat16).reshape(count * SLOT_ROWS, tokens) for a in (chosen, weighted)
    )


def local(queries, cache, lengths, hidden_rows, routes, gate_codes, placement, w_gate_up, w_down):
    sec = lax.axis_index("sec")
    x = cube_exchange(outgoing_rows(hidden_rows, routes, gate_codes), FIRST)

    columns = columns_of_cube()
    slots = jnp.stack([sec * 16 + columns, (1 - sec) * 16 + columns], axis=1).reshape(-1)
    expert_ids = lax.broadcasted_iota(jnp.int32, (2 * CUBE, EXPERTS), 1)
    experts = jnp.sum(jnp.where(placement[None, :] == slots[:, None], expert_ids, 0), axis=1)
    onehot, factors = picks_of(x[:, D:], experts)
    sent = jnp.dot(onehot, x[:, :D], preferred_element_type=jnp.float32).astype(jnp.bfloat16)
    arrived = cube_exchange(sent, SECOND).reshape(CUBE, 2, SLOT_ROWS, D)
    context = attend(queries, cache, lengths)

    count = CUBE * SLOT_ROWS
    gate_act = up_act = None
    for i in range(2):
        cols = slice(EDGES[i], EDGES[i + 1])
        mine, others = (arrived[:, k, :, cols].reshape(count, -1) for k in range(2))
        work = jnp.concatenate([mine, swap_cores(others)])
        if i > 0:
            work, gate_act, up_act = lax.optimization_barrier((work, gate_act, up_act))
        gate = jnp.dot(work, w_gate_up[0, cols], preferred_element_type=jnp.float32)
        up = jnp.dot(work, w_gate_up[1, cols], preferred_element_type=jnp.float32)
        gate_act = gate if gate_act is None else gate_act + gate
        up_act = up if up_act is None else up_act + up
    inner_act = (jax.nn.silu(gate_act) * up_act).astype(jnp.bfloat16)

    back = jnp.zeros((CUBE, 2, SLOT_ROWS, D), jnp.bfloat16)
    for i in range(3):
        partial = jnp.dot(
            inner_act, w_down[:, OUT_EDGES[i] : OUT_EDGES[i + 1]], preferred_element_type=jnp.float32
        ).astype(jnp.bfloat16)
        partial, inner_act = lax.optimization_barrier((partial, inner_act))
        others, inner_act = lax.optimization_barrier((partial[count:], inner_act))
        for k, rows in enumerate((partial[:count], swap_cores(others))):
            back = lax.dynamic_update_slice(
                back, rows.reshape(CUBE, 1, SLOT_ROWS, -1), (0, k, 0, OUT_EDGES[i])
            )
    returned = cube_exchange(back.reshape(2 * count, D), SECOND)
    terms = jnp.einsum("rt,rd->td", factors, returned, preferred_element_type=jnp.float32)
    sums = cube_exchange(terms.astype(jnp.bfloat16), FIRST).reshape(CUBE, ROWS, D)
    mixed = jnp.sum(sums.astype(jnp.float32), axis=0).astype(jnp.bfloat16)
    return (context, mixed)


def solution(mesh):
    return jax.shard_map(
        local,
        mesh=mesh,
        in_specs=(
            P("dev", "sec", None),
            P("dev", None, None),
            P("dev"),
            P(("sec", "dev"), None),
            P(("sec", "dev"), None),
            P(("sec", "dev"), None),
            P(),
            P(None, None, ("sec", "dev")),
            P(("sec", "dev"), None),
        ),
        out_specs=(P("dev", "sec", None), P(("sec", "dev"), None)),
        check_vma=False,
    )
```

profile of v0, /device:TPU:1, one launch (start us, length us, event | category | flops | bytes accessed | tf_op | source)
XLA Modules:
  0.0 147.7 jit_solution(11684230027832460161)
XLA Ops:
  0.6 2.1 %shard_map.122 = bf16[64,7296]{1,0:T(8,128)(2,1)} custom-call(bf16[8,7168]{1,0:T(8,128)(2,1)} %hidden_ref.1, s32[8,8]{1,0:T(8,128)} %routes_ref.1, s32[8,8]{1,0:T(8,128)} %codes_ref.1), custom_call_target="tpu_custom_call" | custom-call | tf_op jit(solution)/shard_map/pallas_call | solution.py:89
  2.8 5.9 %all-to-all-start = ((bf16[8,8,7296]{2,1,0:T(8,128)(2,1)}), bf16[8,8,7296]{2,1,0:T(8,128)(2,1)S(1)}, u32[]{:S(2)}, u32[]{:S(2)}) async-start(bf16[8,8,7296]{2,1,0:T(8,128)(2,1)} %bitcast.78), calls=%async_computation | async-start | bytes 1867776 | tf_op jit(solution)/shard_map/all_to_all | solution.py:46
  8.7 0.7 broadcast_select_fusion
  9.4 0.6 slice.70
  10.6 0.7 add_bitcast_fusion.1
  12.1 0.8 select_reduce_fusion
  13.0 5.6 %all-to-all-done = bf16[8,8,7296]{2,1,0:T(8,128)(2,1)S(1)} async-done(((bf16[8,8,7296]{2,1,0:T(8,128)(2,1)}), bf16[8,8,7296]{2,1,0:T(8,128)(2,1)S(1)}, u32[]{:S(2)}, u32[]{:S(2)}) %all-to-all-start) | async-done | bytes 933920 | tf_op jit(solution)/shard_map/all_to_all | solution.py:46
  18.6 0.2 fusion.29
  18.8 0.4 fusion.28
  19.2 1.6 %convolution_convert_fusion = bf16[384,7168]{1,0:T(8,128)(2,1)S(1)} fusion(pred[384,64]{1,0:T(32,128)(4,1)S(1)} %fusion.28, bf16[64,7296]{1,0:T(8,128)(2,1)S(1)} %bitcast.80), kind=kOutput, calls=%fused_computation.1 | convolution fusion | flops 355074048 | bytes 6471680 | tf_op jit(solution)/shard_map/dot_general | solution.py:137
  20.8 42.4 %all_to_all.42 = bf16[8,48,7168]{2,1,0:T(8,128)(2,1)S(1)} all-to-all(bf16[8,48,7168]{2,1,0:T(8,128)(2,1)S(1)} %bitcast.71), channel_id=1, replica_groups={{0,12,16,28,4,8,20,24},{1,13,17,29,5,9,21,25},{3,15,19,31,7,11,23,27},{..., dimensions={0} | all-to-all | bytes 11010048 | tf_op jit(solution)/shard_map/all_to_all | solution.py:46
  63.3 0.1 fusion.37
  63.4 1.9 %collective-permute-start.1 = (bf16[192,2560]{1,0:T(8,128)(2,1)S(1)}, bf16[192,2560]{1,0:T(8,128)(2,1)S(1)}, u32[]{:S(2)}, u32[]{:S(2)}) collective-permute-start(bf16[192,2560]{1,0:T(8,128)(2,1)S(1)} %bitcast.85), channel_id=1, source_target_pairs={{0,64},{64,0},{1,65},{65,1},{2,66},{66,2},{3,67},{67,3},{4,68},{68... | collective-permute-start | bytes 2949128 | tf_op jit(solution)/shard_map/ppermute | solution.py:50
  65.3 0.2 fusion.38
  65.6 1.9 %collective-permute-done.1 = bf16[192,2560]{1,0:T(8,128)(2,1)S(1)} collective-permute-done((bf16[192,2560]{1,0:T(8,128)(2,1)S(1)}, bf16[192,2560]{1,0:T(8,128)(2,1)S(1)}, u32[]{:S(2)}, u32[]{:S(2)}) %collective-permute-start.1) | collective-permute-done | bytes 983072 | tf_op jit(solution)/shard_map/ppermute | solution.py:50
  67.5 1.2 fusion.10
  68.7 1.2 fusion.8
  69.8 0.2 collective-permute-done
  70.0 0.2 pad_maximum_fusion
  70.2 2.0 %fusion.2 = f32[384,512]{1,0:T(8,128)S(1)} fusion(bf16[384,4608]{1,0:T(8,128)(2,1)S(1)} %pad_maximum_fusion, bf16[2,7168,512]{2,1,0:T(8,128)(2,1)S(1)} %bitcast.91), kind=kOutput, calls=%fused_computation.4 | convolution fusion | flops 1811939328 | bytes 9043968 | tf_op jit(solution)/shard_map/dot_general | solution.py:150
  72.2 2.0 %fusion.4 = f32[384,512]{1,0:T(8,128)S(1)} fusion(bf16[384,4608]{1,0:T(8,128)(2,1)S(1)} %pad_maximum_fusion, bf16[2,7168,512]{2,1,0:T(8,128)(2,1)S(1)} %bitcast.91), kind=kOutput, calls=%fused_computation.6 | convolution fusion | flops 1811939328 | bytes 9043968 | tf_op jit(solution)/shard_map/dot_general | solution.py:149
  74.2 0.4 multiply_convert_fusion
  74.7 1.1 convolution_convert_fusion.2
  75.8 0.1 fusion.41
  75.9 0.5 collective-permute-start.2
  76.4 1.2 convolution_convert_fusion.4
  77.6 0.1 fusion.40
  77.7 0.2 collective-permute-start.3
  78.0 1.2 convolution_convert_fusion.3
  79.2 0.1 fusion.39
  79.3 0.6 collective-permute-start.4
  80.0 0.6 dynamic_update_slice.18
  80.7 0.1 constant_dynamic-update-slice_fusion.3
  80.9 0.1 constant_dynamic-update-slice_fusion.2
  81.0 0.1 constant_dynamic-update-slice_fusion.1
  81.1 1.0 collective-permute-done.4
  82.1 0.1 constant_dynamic-update-slice_fusion
  82.2 2.5 %copy-done.1 = bf16[8,2,24,7168]{3,2,1,0:T(8,128)(2,1)} copy-done((bf16[8,2,24,7168]{3,2,1,0:T(8,128)(2,1)}, bf16[8,2,24,7168]{3,2,1,0:T(8,128)(2,1)S(1)}, u32[]{:S(2)}) %copy-start.1) | copy-done | bytes 5505048
  84.7 4.7 %all-to-all-start.2 = ((bf16[8,48,7168]{2,1,0:T(8,128)(2,1)}), bf16[8,48,7168]{2,1,0:T(8,128)(2,1)}, u32[]{:S(2)}, u32[]{:S(2)}) async-start(bf16[8,48,7168]{2,1,0:T(8,128)(2,1)} %bitcast.74), calls=%async_computation.2 | async-start | bytes 11010048 | tf_op jit(solution)/shard_map/all_to_all | solution.py:46
  89.4 0.1 select_convert_fusion
  89.5 39.4 %all-to-all-done.2 = bf16[8,48,7168]{2,1,0:T(8,128)(2,1)} async-done(((bf16[8,48,7168]{2,1,0:T(8,128)(2,1)}), bf16[8,48,7168]{2,1,0:T(8,128)(2,1)}, u32[]{:S(2)}, u32[]{:S(2)}) %all-to-all-start.2) | async-done | bytes 5505056 | tf_op jit(solution)/shard_map/all_to_all | solution.py:46
  128.9 4.6 %fusion.1 = bf16[8,8,7168]{2,1,0:T(8,128)(2,1)} fusion(bf16[384,64]{1,0:T(8,128)(2,1)S(1)} %bitcast.89, bf16[384,7168]{1,0:T(8,128)(2,1)} %bitcast.33), kind=kOutput, calls=%fused_computation.3 | convolution fusion | flops 352780288 | bytes 6471680 | tf_op jit(solution)/shard_map/rt,rd->td/dot_general | solution.py:167
  133.5 3.6 %all-to-all-start.3 = ((bf16[8,8,7168]{2,1,0:T(8,128)(2,1)}), bf16[8,8,7168]{2,1,0:T(8,128)(2,1)S(1)}, u32[]{:S(2)}, u32[]{:S(2)}) async-start(bf16[8,8,7168]{2,1,0:T(8,128)(2,1)} %fusion.1), calls=%async_computation.3 | async-start | bytes 1835008 | tf_op jit(solution)/shard_map/all_to_all | solution.py:46
  137.1 2.2 %fusion.24 = f32[8,64,256]{2,1,0:T(8,128)S(1)} fusion(bf16[8,64,576]{2,1,0:T(8,128)(2,1)S(1)} %copy-done, bf16[8,256,576]{1,2,0:T(8,128)(2,1)} %param.12, s32[8]{0:T(128)S(1)} %copy-done.2), kind=kOutput, calls=%fused_computation.30 | convolution fusion | flops 151388160 | bytes 3473440 | tf_op jit(solution)/shard_map/rhc,rlc->rhl/dot_general | solution.py:55
  139.3 0.2 fusion.42
  139.5 3.4 %fusion.19 = bf16[8,64,512]{2,1,0:T(8,128)(2,1)} fusion(bf16[8,256,576]{1,2,0:T(8,128)(2,1)} %param.12, f32[8,64]{1,0:T(8,128)S(1)} %fusion.42, f32[8,64,256]{2,1,0:T(8,128)S(1)} %fusion.24), kind=kOutput, calls=%fused_computation.26 | convolution fusion | flops 134873856 | bytes 3674112 | tf_op jit(solution)/shard_map/rhl,rlc->rhc/dot_general | solution.py:62
  142.9 4.0 %all-to-all-done.3 = bf16[8,8,7168]{2,1,0:T(8,128)(2,1)S(1)} async-done(((bf16[8,8,7168]{2,1,0:T(8,128)(2,1)}), bf16[8,8,7168]{2,1,0:T(8,128)(2,1)S(1)}, u32[]{:S(2)}, u32[]{:S(2)}) %all-to-all-start.3) | async-done | bytes 917536 | tf_op jit(solution)/shard_map/all_to_all | solution.py:46
  146.9 0.8 reduce_sum.32
  (49 shorter events, 1.1 us)
Async XLA Ops:
  0.6 136.4 %copy-start = (bf16[8,64,576]{2,1,0:T(8,128)(2,1)S(1)}, bf16[8,64,576]{2,1,0:T(8,128)(2,1)}, u32[]{:S(2)}) copy-start(bf16[8,64,576]{2,1,0:T(8,128)(2,1)} %param.11) | copy-start | bytes 1769476
  2.8 15.9 %all-to-all-start = ((bf16[8,8,7296]{2,1,0:T(8,128)(2,1)}), bf16[8,8,7296]{2,1,0:T(8,128)(2,1)S(1)}, u32[]{:S(2)}, u32[]{:S(2)}) async-start(bf16[8,8,7296]{2,1,0:T(8,128)(2,1)} %bitcast.78), calls=%async_computation | async-start | bytes 1867776 | tf_op jit(solution)/shard_map/all_to_all | solution.py:46
  19.2 48.3 %slice-start = ((s8[14680064]{0:T(1024)(128)(4,1)}), s8[4194304]{0:T(1024)(128)(4,1)S(1)}, s32[]{:S(2)}) async-start(s8[14680064]{0:T(1024)(128)(4,1)} %bitcast.90), calls=%async_computation.4 | async-start | bytes 8388608
  19.2 48.2 %slice-start.1 = ((s8[14680064]{0:T(1024)(128)(4,1)}), s8[4194304]{0:T(1024)(128)(4,1)S(1)}, s32[]{:S(2)}) async-start(s8[14680064]{0:T(1024)(128)(4,1)} %bitcast.90), calls=%async_computation.5 | async-start | bytes 8388608
  20.8 46.7 %slice-start.2 = ((s8[14680064]{0:T(1024)(128)(4,1)}), s8[4194304]{0:T(1024)(128)(4,1)S(1)}, s32[]{:S(2)}) async-start(s8[14680064]{0:T(1024)(128)(4,1)} %bitcast.90), calls=%async_computation.6 | async-start | bytes 8388608
  63.2 4.2 %slice-start.3 = ((s8[14680064]{0:T(1024)(128)(4,1)}), s8[2097152]{0:T(1024)(128)(4,1)S(1)}, s32[]{:S(2)}) async-start(s8[14680064]{0:T(1024)(128)(4,1)} %bitcast.90), calls=%async_computation.7 | async-start | bytes 4194304
  63.4 4.1 %collective-permute-start.1 = (bf16[192,2560]{1,0:T(8,128)(2,1)S(1)}, bf16[192,2560]{1,0:T(8,128)(2,1)S(1)}, u32[]{:S(2)}, u32[]{:S(2)}) collective-permute-start(bf16[192,2560]{1,0:T(8,128)(2,1)S(1)} %bitcast.85), channel_id=1, source_target_pairs={{0,64},{64,0},{1,65},{65,1},{2,66},{66,2},{3,67},{67,3},{4,68},{68... | collective-permute-start | bytes 2949128 | tf_op jit(solution)/shard_map/ppermute | solution.py:50
  65.5 4.5 %collective-permute-start = (bf16[192,4608]{1,0:T(8,128)(2,1)S(1)}, bf16[192,4608]{1,0:T(8,128)(2,1)S(1)}, u32[]{:S(2)}, u32[]{:S(2)}) collective-permute-start(bf16[192,4608]{1,0:T(8,128)(2,1)S(1)} %bitcast.82), channel_id=1, source_target_pairs={{0,64},{64,0},{1,65},{65,1},{2,66},{66,2},{3,67},{67,3},{4,68},{68... | collective-permute-start | bytes 5308424 | tf_op jit(solution)/shard_map/ppermute | solution.py:50
  70.2 4.4 %slice-start.4 = ((s8[7340032]{0:T(1024)(128)(4,1)}), s8[4194304]{0:T(1024)(128)(4,1)S(1)}, s32[]{:S(2)}) async-start(s8[7340032]{0:T(1024)(128)(4,1)} %bitcast.92), calls=%async_computation.8 | async-start | bytes 8388608
  72.2 2.4 %slice-start.5 = ((s8[7340032]{0:T(1024)(128)(4,1)}), s8[3145728]{0:T(1024)(128)(4,1)S(1)}, s32[]{:S(2)}) async-start(s8[7340032]{0:T(1024)(128)(4,1)} %bitcast.92), calls=%async_computation.9 | async-start | bytes 6291456
  75.9 4.7 %collective-permute-start.2 = (bf16[192,2304]{1,0:T(8,128)(2,1)S(1)}, bf16[192,2304]{1,0:T(8,128)(2,1)S(1)}, u32[]{:S(2)}, u32[]{:S(2)}) collective-permute-start(bf16[192,2304]{1,0:T(8,128)(2,1)S(1)} %get-tuple-element.19), channel_id=1, source_target_pairs={{0,64},{64,0},{1,65},{65,1},{2,66},{66,2},{3,67},{67,3},{4,68},{68... | collective-permute-start | bytes 2654216 | tf_op jit(solution)/shard_map/ppermute | solution.py:50
  77.7 3.1 %collective-permute-start.3 = (bf16[192,2432]{1,0:T(8,128)(2,1)S(1)}, bf16[192,2432]{1,0:T(8,128)(2,1)S(1)}, u32[]{:S(2)}, u32[]{:S(2)}) collective-permute-start(bf16[192,2432]{1,0:T(8,128)(2,1)S(1)} %get-tuple-element.23), channel_id=1, source_target_pairs={{0,64},{64,0},{1,65},{65,1},{2,66},{66,2},{3,67},{67,3},{4,68},{68... | collective-permute-start | bytes 2801672 | tf_op jit(solution)/shard_map/ppermute | solution.py:50
  79.3 2.8 %collective-permute-start.4 = (bf16[192,2432]{1,0:T(8,128)(2,1)S(1)}, bf16[192,2432]{1,0:T(8,128)(2,1)S(1)}, u32[]{:S(2)}, u32[]{:S(2)}) collective-permute-start(bf16[192,2432]{1,0:T(8,128)(2,1)S(1)} %get-tuple-element.32), channel_id=1, source_target_pairs={{0,64},{64,0},{1,65},{65,1},{2,66},{66,2},{3,67},{67,3},{4,68},{68... | collective-permute-start | bytes 2801672 | tf_op jit(solution)/shard_map/ppermute | solution.py:50
  82.2 2.5 %copy-start.1 = (bf16[8,2,24,7168]{3,2,1,0:T(8,128)(2,1)}, bf16[8,2,24,7168]{3,2,1,0:T(8,128)(2,1)S(1)}, u32[]{:S(2)}) copy-start(bf16[8,2,24,7168]{3,2,1,0:T(8,128)(2,1)S(1)} %constant_dynamic-update-slice_fusion) | copy-start | bytes 16515076
  84.7 44.2 %all-to-all-start.2 = ((bf16[8,48,7168]{2,1,0:T(8,128)(2,1)}), bf16[8,48,7168]{2,1,0:T(8,128)(2,1)}, u32[]{:S(2)}, u32[]{:S(2)}) async-start(bf16[8,48,7168]{2,1,0:T(8,128)(2,1)} %bitcast.74), calls=%async_computation.2 | async-start | bytes 11010048 | tf_op jit(solution)/shard_map/all_to_all | solution.py:46
  128.9 8.1 %copy-start.2 = (s32[8]{0:T(128)S(1)}, s32[8]{0:T(128)}, u32[]{:S(2)}) copy-start(s32[8]{0:T(128)} %param.13) | copy-start | bytes 100
  133.5 13.4 %all-to-all-start.3 = ((bf16[8,8,7168]{2,1,0:T(8,128)(2,1)}), bf16[8,8,7168]{2,1,0:T(8,128)(2,1)S(1)}, u32[]{:S(2)}, u32[]{:S(2)}) async-start(bf16[8,8,7168]{2,1,0:T(8,128)(2,1)} %fusion.1), calls=%async_computation.3 | async-start | bytes 1835008 | tf_op jit(solution)/shard_map/all_to_all | solution.py:46
where the time goes:
time: 148 us
  waiting for transfers between devices  52 us (35%)
  blocking collectives  42.4 us (29%)
  matrix products  21.8 us (15%)
  starting transfers between devices  17.4 us (12%)
  local copies, waits for them, and re-layouts  5.78 us (4%)
  other arithmetic  4.48 us (3%)
  Pallas kernels  2.1 us (1%)
  between operations  1.75 us (1%)
    all_to_all x3, waiting for transfers between devices, cube_exchange(): lax.all_to_all(rows, AXES, 0, 0, tiled=True, axis_index_groups=groups)  49 us
    all_to_all x1, blocking collectives, cube_exchange(): lax.all_to_all(rows, AXES, 0, 0, tiled=True, axis_index_groups=groups)  42.4 us
    all_to_all x3, starting transfers between devices, cube_exchange(): lax.all_to_all(rows, AXES, 0, 0, tiled=True, axis_index_groups=groups)  14.1 us
    dot_general x1, matrix products, local(): jnp.einsum('rt,rd->td', factors, returned, preferred_element_type=jnp.flo...  4.56 us
    dot_general x3, matrix products, local(): jnp.dot(inner_act, w_down[:, OUT_EDGES[i]:OUT_EDGES[i + 1]], preferred_el...  3.55 us
    dot_general x1, matrix products, attend(): jnp.einsum('rhl,rlc->rhc', weights, cache[:, :, :LATENT], preferred_eleme...  3.4 us
    ppermute x5, starting transfers between devices, swap_cores(): return lax.ppermute(rows, 'sec', [(0, 1), (1, 0)])  3.29 us
    dot_general x2, matrix products, local(): up = jnp.dot(work, w_gate_up[1, cols], preferred_element_type=jnp.float32)  3.15 us
  transfers between devices with their start and end apart: 8, of which 6 were waited for; matrix products, arithmetic and copies ran while one was open for 11% of the time, Pallas kernels for 0%

commit v1 on v0

--- a/solution.py
+++ b/solution.py
@@ -2,6 +2,7 @@
 import jax.numpy as jnp
 from jax import lax
 from jax.experimental import pallas as pl
+from jax.experimental.pallas import tpu as pltpu
 from jax.sharding import PartitionSpec as P
 
 D = 7168
@@ -20,7 +21,7 @@
 TABLE = 128
 SLOT_ROWS = 24
 EDGES = (0, 2560, 7168)
-OUT_EDGES = (0, 2304, 4736, 7168)
+OUT_EDGES = (0, 2816, 5632, 7168)
 
 
 def code_of(dev):
@@ -125,6 +126,28 @@
     )
 
 
+def spread_kernel(factors_ref, rows_ref, out_ref):
+    out_ref[...] = jnp.dot(
+        factors_ref[...], rows_ref[...], preferred_element_type=jnp.float32
+    ).astype(out_ref.dtype)
+
+
+def spread(factors, rows):
+    tokens, count = factors.shape
+    block = rows.shape[1] // 2
+    return pl.pallas_call(
+        spread_kernel,
+        grid=(2,),
+        in_specs=[
+            pl.BlockSpec((tokens, count), lambda n: (0, 0)),
+            pl.BlockSpec((count, block), lambda n: (0, n)),
+        ],
+        out_specs=pl.BlockSpec((tokens, block), lambda n: (0, n)),
+        out_shape=jax.ShapeDtypeStruct((tokens, rows.shape[1]), jnp.bfloat16),
+        compiler_params=pltpu.CompilerParams(vmem_limit_bytes=60 * 2**20),
+    )(factors, rows)
+
+
 def local(queries, cache, lengths, hidden_rows, routes, gate_codes, placement, w_gate_up, w_down):
     sec = lax.axis_index("sec")
     x = cube_exchange(outgoing_rows(hidden_rows, routes, gate_codes), FIRST)
@@ -164,8 +187,8 @@
                 back, rows.reshape(CUBE, 1, SLOT_ROWS, -1), (0, k, 0, OUT_EDGES[i])
             )
     returned = cube_exchange(back.reshape(2 * count, D), SECOND)
-    terms = jnp.einsum("rt,rd->td", factors, returned, preferred_element_type=jnp.float32)
-    sums = cube_exchange(terms.astype(jnp.bfloat16), FIRST).reshape(CUBE, ROWS, D)
+    terms = spread(factors.T, returned)
+    sums = cube_exchange(terms, FIRST).reshape(CUBE, ROWS, D)
     mixed = jnp.sum(sums.astype(jnp.float32), axis=0).astype(jnp.bfloat16)
     return (context, mixed)
 

time: 148 us -> 147 us (level)
  matrix products: 21.8 us -> 17.2 us
  Pallas kernels: 2.1 us -> 6.13 us
    dot_general x1 -> x0, matrix products: 4.56 us -> none  [local(): jnp.einsum('rt,rd->td', factors, returned, preferred_element_type=jnp.flo...]
    pallas_call x0 -> x1, Pallas kernels: none -> 4.03 us  [spread(): pl.pallas_call(spread_kernel, grid=(2,), in_specs=[pl.BlockSpec((tokens,...]
    dynamic_update_slice x6 -> x7, local copies, waits for them, and re-layouts: 1.23 us -> 4 us  [local(): lax.dynamic_update_slice(back, rows.reshape(CUBE, 1, SLOT_ROWS, -1), (0,...]
    unnamed x18 -> x16, local copies, waits for them, and re-layouts: 2.51 us -> 0.05 us
  transfers between devices with their start and end apart: 8 -> 8, of which waited for: 6 -> 7; matrix products, arithmetic and copies ran while one was open for 11% -> 11% of each run, Pallas kernels for 0% -> 0%
where the time goes in v1:
time: 147 us
  waiting for transfers between devices  51.1 us (35%)
  blocking collectives  42.4 us (29%)
  starting transfers between devices  17.4 us (12%)
  matrix products  17.2 us (12%)
  local copies, waits for them, and re-layouts  6.32 us (4%)
  Pallas kernels  6.13 us (4%)
  other arithmetic  4.72 us (3%)
  between operations  1.74 us (1%)
    all_to_all x3, waiting for transfers between devices, cube_exchange(): lax.all_to_all(rows, AXES, 0, 0, tiled=True, axis_index_groups=groups)  48.3 us
    all_to_all x1, blocking collectives, cube_exchange(): lax.all_to_all(rows, AXES, 0, 0, tiled=True, axis_index_groups=groups)  42.4 us
    all_to_all x3, starting transfers between devices, cube_exchange(): lax.all_to_all(rows, AXES, 0, 0, tiled=True, axis_index_groups=groups)  14.1 us
    pallas_call x1, Pallas kernels, spread(): pl.pallas_call(spread_kernel, grid=(2,), in_specs=[pl.BlockSpec((tokens,...  4.03 us
    dynamic_update_slice x7, local copies, waits for them, and re-layouts, local(): lax.dynamic_update_slice(back, rows.reshape(CUBE, 1, SLOT_ROWS, -1), (0,...  4 us
    dot_general x1, matrix products, attend(): jnp.einsum('rhl,rlc->rhc', weights, cache[:, :, :LATENT], preferred_eleme...  3.4 us
    dot_general x3, matrix products, local(): jnp.dot(inner_act, w_down[:, OUT_EDGES[i]:OUT_EDGES[i + 1]], preferred_el...  3.35 us
    ppermute x5, starting transfers between devices, swap_cores(): return lax.ppermute(rows, 'sec', [(0, 1), (1, 0)])  3.29 us
  transfers between devices with their start and end apart: 8, of which 7 were waited for; matrix products, arithmetic and copies ran while one was open for 11% of the time, Pallas kernels for 0%

profile of v1, /device:TPU:1, one launch (start us, length us, event | category | flops | bytes accessed | tf_op | source)
XLA Modules:
  0.0 147.0 jit_solution(9379362948044025479)
XLA Ops:
  0.6 2.1 %shard_map.122 = bf16[64,7296]{1,0:T(8,128)(2,1)} custom-call(bf16[8,7168]{1,0:T(8,128)(2,1)} %hidden_ref.1, s32[8,8]{1,0:T(8,128)} %routes_ref.1, s32[8,8]{1,0:T(8,128)} %codes_ref.1), custom_call_target="tpu_custom_call" | custom-call | tf_op jit(solution)/shard_map/pallas_call | solution.py:90
  2.7 5.9 %all-to-all-start = ((bf16[8,8,7296]{2,1,0:T(8,128)(2,1)}), bf16[8,8,7296]{2,1,0:T(8,128)(2,1)S(1)}, u32[]{:S(2)}, u32[]{:S(2)}) async-start(bf16[8,8,7296]{2,1,0:T(8,128)(2,1)} %bitcast.61), calls=%async_computation | async-start | bytes 1867776 | tf_op jit(solution)/shard_map/all_to_all | solution.py:47
  8.7 0.7 broadcast_select_fusion
  9.4 0.6 slice.70
  10.6 0.7 add_bitcast_fusion.1
  12.1 0.8 select_reduce_fusion
  13.0 5.6 %all-to-all-done = bf16[8,8,7296]{2,1,0:T(8,128)(2,1)S(1)} async-done(((bf16[8,8,7296]{2,1,0:T(8,128)(2,1)}), bf16[8,8,7296]{2,1,0:T(8,128)(2,1)S(1)}, u32[]{:S(2)}, u32[]{:S(2)}) %all-to-all-start) | async-done | bytes 933920 | tf_op jit(solution)/shard_map/all_to_all | solution.py:47
  18.6 0.2 fusion.28
  18.8 0.1 copy.25
  19.0 1.7 %convolution_convert_fusion = bf16[384,7168]{1,0:T(8,128)(2,1)S(1)} fusion(bf16[64,7296]{1,0:T(8,128)(2,1)S(1)} %bitcast.63, f32[384,64]{0,1:T(8,128)S(1)} %copy.25, s32[384]{0:T(512)S(1)} %iota.91, s32[384]{0:T(512)S(1)} %iota.88, s32[64]{0:T(128)S(1)} %get-tuple-element.40, s32[64]{0:T(128)S(1)} %get-tuple-element.41, s32[384]{0:T(512)S(1)} %iota.76, ...), kind=kOutput, calls=%fused_computation.1 | convolution fusion | flops 355270656 | bytes 6531584 | tf_op jit(solution)/shard_map/dot_general | solution.py:160
  20.7 42.4 %all_to_all.41 = bf16[8,48,7168]{2,1,0:T(8,128)(2,1)S(1)} all-to-all(bf16[8,48,7168]{2,1,0:T(8,128)(2,1)S(1)} %bitcast.54), channel_id=1, replica_groups={{0,12,16,28,4,8,20,24},{1,13,17,29,5,9,21,25},{3,15,19,31,7,11,23,27},{..., dimensions={0} | all-to-all | bytes 11010048 | tf_op jit(solution)/shard_map/all_to_all | solution.py:47
  63.1 0.1 fusion.37
  63.3 1.9 %collective-permute-start.1 = (bf16[192,2560]{1,0:T(8,128)(2,1)S(1)}, bf16[192,2560]{1,0:T(8,128)(2,1)S(1)}, u32[]{:S(2)}, u32[]{:S(2)}) collective-permute-start(bf16[192,2560]{1,0:T(8,128)(2,1)S(1)} %bitcast.71), channel_id=1, source_target_pairs={{0,64},{64,0},{1,65},{65,1},{2,66},{66,2},{3,67},{67,3},{4,68},{68... | collective-permute-start | bytes 2949128 | tf_op jit(solution)/shard_map/ppermute | solution.py:51
  65.2 0.2 fusion.38
  65.5 1.9 %collective-permute-done.1 = bf16[192,2560]{1,0:T(8,128)(2,1)S(1)} collective-permute-done((bf16[192,2560]{1,0:T(8,128)(2,1)S(1)}, bf16[192,2560]{1,0:T(8,128)(2,1)S(1)}, u32[]{:S(2)}, u32[]{:S(2)}) %collective-permute-start.1) | collective-permute-done | bytes 983072 | tf_op jit(solution)/shard_map/ppermute | solution.py:51
  67.4 1.2 fusion.11
  68.6 1.2 fusion.9
  69.7 0.2 collective-permute-done
  69.9 0.2 pad_maximum_fusion
  70.1 2.0 %fusion.1 = f32[384,512]{1,0:T(8,128)S(1)} fusion(bf16[384,4608]{1,0:T(8,128)(2,1)S(1)} %pad_maximum_fusion, bf16[2,7168,512]{2,1,0:T(8,128)(2,1)S(1)} %bitcast.76), kind=kOutput, calls=%fused_computation.2 | convolution fusion | flops 1811939328 | bytes 9043968 | tf_op jit(solution)/shard_map/dot_general | solution.py:173
  72.1 2.0 %fusion.3 = f32[384,512]{1,0:T(8,128)S(1)} fusion(bf16[384,4608]{1,0:T(8,128)(2,1)S(1)} %pad_maximum_fusion, bf16[2,7168,512]{2,1,0:T(8,128)(2,1)S(1)} %bitcast.76), kind=kOutput, calls=%fused_computation.4 | convolution fusion | flops 1811939328 | bytes 9043968 | tf_op jit(solution)/shard_map/dot_general | solution.py:172
  74.1 0.4 multiply_convert_fusion
  74.6 1.3 convolution_convert_fusion.2
  75.9 0.1 fusion.40
  76.0 0.5 collective-permute-start.2
  76.5 1.3 convolution_convert_fusion.1
  77.8 0.1 fusion.39
  77.9 0.2 collective-permute-start.3
  78.1 0.8 convolution_convert_fusion.3
  79.0 0.6 collective-permute-start.4
  79.6 0.6 dynamic_update_slice.18
  80.3 0.1 constant_dynamic-update-slice_fusion.4
  80.4 0.1 constant_dynamic-update-slice_fusion.3
  80.5 0.2 collective-permute-done.3
  80.7 0.1 constant_dynamic-update-slice_fusion.2
  80.9 0.7 collective-permute-done.4
  81.6 2.9 %copy.27 = bf16[8,2,24,7168]{3,2,1,0:T(8,128)(2,1)} copy(bf16[8,2,24,7168]{3,2,0,1:T(8,128)(2,1)S(1)} %constant_dynamic-update-slice_fusion) | data formatting | bytes 11010048 | tf_op jit(solution)/shard_map/dynamic_update_slice | solution.py:186
  84.5 4.7 %all-to-all-start.2 = ((bf16[8,48,7168]{2,1,0:T(8,128)(2,1)}), bf16[8,48,7168]{2,1,0:T(8,128)(2,1)}, u32[]{:S(2)}, u32[]{:S(2)}) async-start(bf16[8,48,7168]{2,1,0:T(8,128)(2,1)} %bitcast.55), calls=%async_computation.2 | async-start | bytes 11010048 | tf_op jit(solution)/shard_map/all_to_all | solution.py:47
  89.3 0.1 copy.26
  89.4 0.7 fusion.27.factors_ref
  90.1 38.7 %all-to-all-done.2 = bf16[8,48,7168]{2,1,0:T(8,128)(2,1)} async-done(((bf16[8,48,7168]{2,1,0:T(8,128)(2,1)}), bf16[8,48,7168]{2,1,0:T(8,128)(2,1)}, u32[]{:S(2)}, u32[]{:S(2)}) %all-to-all-start.2) | async-done | bytes 5505056 | tf_op jit(solution)/shard_map/all_to_all | solution.py:47
  128.7 4.0 %shard_map.123 = bf16[64,7168]{1,0:T(8,128)(2,1)} custom-call(bf16[64,384]{1,0:T(8,128)(2,1)} %fusion.27.factors_ref, bf16[384,7168]{1,0:T(8,128)(2,1)} %bitcast.28.rows_ref), custom_call_target="tpu_custom_call" | custom-call | tf_op jit(solution)/shard_map/pallas_call | solution.py:138
  132.8 3.6 %all-to-all-start.3 = ((bf16[8,8,7168]{2,1,0:T(8,128)(2,1)}), bf16[8,8,7168]{2,1,0:T(8,128)(2,1)S(1)}, u32[]{:S(2)}, u32[]{:S(2)}) async-start(bf16[8,8,7168]{2,1,0:T(8,128)(2,1)} %bitcast.64), calls=%async_computation.3 | async-start | bytes 1835008 | tf_op jit(solution)/shard_map/all_to_all | solution.py:47
  136.4 2.2 %fusion.23 = f32[8,64,256]{2,1,0:T(8,128)S(1)} fusion(bf16[8,64,576]{2,1,0:T(8,128)(2,1)S(1)} %copy-done, bf16[8,256,576]{1,2,0:T(8,128)(2,1)} %param.12, s32[8]{0:T(128)S(1)} %copy-done.1), kind=kOutput, calls=%fused_computation.28 | convolution fusion | flops 151388160 | bytes 3473440 | tf_op jit(solution)/shard_map/rhc,rlc->rhl/dot_general | solution.py:56
  138.6 0.2 fusion.42
  138.8 3.4 %fusion.18 = bf16[8,64,512]{2,1,0:T(8,128)(2,1)} fusion(bf16[8,256,576]{1,2,0:T(8,128)(2,1)} %param.12, f32[8,64]{1,0:T(8,128)S(1)} %fusion.42, f32[8,64,256]{2,1,0:T(8,128)S(1)} %fusion.23), kind=kOutput, calls=%fused_computation.24 | convolution fusion | flops 134873856 | bytes 3674112 | tf_op jit(solution)/shard_map/rhl,rlc->rhc/dot_general | solution.py:63
  142.2 4.0 %all-to-all-done.3 = bf16[8,8,7168]{2,1,0:T(8,128)(2,1)S(1)} async-done(((bf16[8,8,7168]{2,1,0:T(8,128)(2,1)}), bf16[8,8,7168]{2,1,0:T(8,128)(2,1)S(1)}, u32[]{:S(2)}, u32[]{:S(2)}) %all-to-all-start.3) | async-done | bytes 917536 | tf_op jit(solution)/shard_map/all_to_all | solution.py:47
  146.2 0.8 reduce_sum.32
  (52 shorter events, 1.2 us)
Async XLA Ops:
  0.6 135.7 %copy-start = (bf16[8,64,576]{2,1,0:T(8,128)(2,1)S(1)}, bf16[8,64,576]{2,1,0:T(8,128)(2,1)}, u32[]{:S(2)}) copy-start(bf16[8,64,576]{2,1,0:T(8,128)(2,1)} %param.11) | copy-start | bytes 1769476
  2.7 15.9 %all-to-all-start = ((bf16[8,8,7296]{2,1,0:T(8,128)(2,1)}), bf16[8,8,7296]{2,1,0:T(8,128)(2,1)S(1)}, u32[]{:S(2)}, u32[]{:S(2)}) async-start(bf16[8,8,7296]{2,1,0:T(8,128)(2,1)} %bitcast.61), calls=%async_computation | async-start | bytes 1867776 | tf_op jit(solution)/shard_map/all_to_all | solution.py:47
  19.0 48.4 %slice-start = ((s8[14680064]{0:T(1024)(128)(4,1)}), s8[4194304]{0:T(1024)(128)(4,1)S(1)}, s32[]{:S(2)}) async-start(s8[14680064]{0:T(1024)(128)(4,1)} %bitcast.75), calls=%async_computation.4 | async-start | bytes 8388608
  19.0 48.4 %slice-start.1 = ((s8[14680064]{0:T(1024)(128)(4,1)}), s8[4194304]{0:T(1024)(128)(4,1)S(1)}, s32[]{:S(2)}) async-start(s8[14680064]{0:T(1024)(128)(4,1)} %bitcast.75), calls=%async_computation.5 | async-start | bytes 8388608
  20.7 46.7 %slice-start.2 = ((s8[14680064]{0:T(1024)(128)(4,1)}), s8[4194304]{0:T(1024)(128)(4,1)S(1)}, s32[]{:S(2)}) async-start(s8[14680064]{0:T(1024)(128)(4,1)} %bitcast.75), calls=%async_computation.6 | async-start | bytes 8388608
  63.1 4.2 %slice-start.3 = ((s8[14680064]{0:T(1024)(128)(4,1)}), s8[2097152]{0:T(1024)(128)(4,1)S(1)}, s32[]{:S(2)}) async-start(s8[14680064]{0:T(1024)(128)(4,1)} %bitcast.75), calls=%async_computation.7 | async-start | bytes 4194304
  63.3 4.1 %collective-permute-start.1 = (bf16[192,2560]{1,0:T(8,128)(2,1)S(1)}, bf16[192,2560]{1,0:T(8,128)(2,1)S(1)}, u32[]{:S(2)}, u32[]{:S(2)}) collective-permute-start(bf16[192,2560]{1,0:T(8,128)(2,1)S(1)} %bitcast.71), channel_id=1, source_target_pairs={{0,64},{64,0},{1,65},{65,1},{2,66},{66,2},{3,67},{67,3},{4,68},{68... | collective-permute-start | bytes 2949128 | tf_op jit(solution)/shard_map/ppermute | solution.py:51
  65.4 4.5 %collective-permute-start = (bf16[192,4608]{1,0:T(8,128)(2,1)S(1)}, bf16[192,4608]{1,0:T(8,128)(2,1)S(1)}, u32[]{:S(2)}, u32[]{:S(2)}) collective-permute-start(bf16[192,4608]{1,0:T(8,128)(2,1)S(1)} %bitcast.66), channel_id=1, source_target_pairs={{0,64},{64,0},{1,65},{65,1},{2,66},{66,2},{3,67},{67,3},{4,68},{68... | collective-permute-start | bytes 5308424 | tf_op jit(solution)/shard_map/ppermute | solution.py:51
  70.1 4.4 %slice-start.4 = ((s8[7340032]{0:T(1024)(128)(4,1)}), s8[4194304]{0:T(1024)(128)(4,1)S(1)}, s32[]{:S(2)}) async-start(s8[7340032]{0:T(1024)(128)(4,1)} %bitcast.77), calls=%async_computation.8 | async-start | bytes 8388608
  72.1 2.4 %slice-start.5 = ((s8[7340032]{0:T(1024)(128)(4,1)}), s8[3145728]{0:T(1024)(128)(4,1)S(1)}, s32[]{:S(2)}) async-start(s8[7340032]{0:T(1024)(128)(4,1)} %bitcast.77), calls=%async_computation.9 | async-start | bytes 6291456
  76.0 4.2 %collective-permute-start.2 = (bf16[192,2816]{1,0:T(8,128)(2,1)S(1)}, bf16[192,2816]{1,0:T(8,128)(2,1)S(1)}, u32[]{:S(2)}, u32[]{:S(2)}) collective-permute-start(bf16[192,2816]{1,0:T(8,128)(2,1)S(1)} %get-tuple-element.19), channel_id=1, source_target_pairs={{0,64},{64,0},{1,65},{65,1},{2,66},{66,2},{3,67},{67,3},{4,68},{68... | collective-permute-start | bytes 3244040 | tf_op jit(solution)/shard_map/ppermute | solution.py:51
  77.9 2.8 %collective-permute-start.3 = (bf16[192,2816]{1,0:T(8,128)(2,1)S(1)}, bf16[192,2816]{1,0:T(8,128)(2,1)S(1)}, u32[]{:S(2)}, u32[]{:S(2)}) collective-permute-start(bf16[192,2816]{1,0:T(8,128)(2,1)S(1)} %get-tuple-element.23), channel_id=1, source_target_pairs={{0,64},{64,0},{1,65},{65,1},{2,66},{66,2},{3,67},{67,3},{4,68},{68... | collective-permute-start | bytes 3244040 | tf_op jit(solution)/shard_map/ppermute | solution.py:51
  79.0 2.5 %collective-permute-start.4 = (bf16[192,1536]{1,0:T(8,128)(2,1)S(1)}, bf16[192,1536]{1,0:T(8,128)(2,1)S(1)}, u32[]{:S(2)}, u32[]{:S(2)}) collective-permute-start(bf16[192,1536]{1,0:T(8,128)(2,1)S(1)} %get-tuple-element.36), channel_id=1, source_target_pairs={{0,64},{64,0},{1,65},{65,1},{2,66},{66,2},{3,67},{67,3},{4,68},{68... | collective-permute-start | bytes 1769480 | tf_op jit(solution)/shard_map/ppermute | solution.py:51
  84.5 44.2 %all-to-all-start.2 = ((bf16[8,48,7168]{2,1,0:T(8,128)(2,1)}), bf16[8,48,7168]{2,1,0:T(8,128)(2,1)}, u32[]{:S(2)}, u32[]{:S(2)}) async-start(bf16[8,48,7168]{2,1,0:T(8,128)(2,1)} %bitcast.55), calls=%async_computation.2 | async-start | bytes 11010048 | tf_op jit(solution)/shard_map/all_to_all | solution.py:47
  128.7 7.6 %copy-start.1 = (s32[8]{0:T(128)S(1)}, s32[8]{0:T(128)}, u32[]{:S(2)}) copy-start(s32[8]{0:T(128)} %param.13) | copy-start | bytes 100
  132.8 13.4 %all-to-all-start.3 = ((bf16[8,8,7168]{2,1,0:T(8,128)(2,1)}), bf16[8,8,7168]{2,1,0:T(8,128)(2,1)S(1)}, u32[]{:S(2)}, u32[]{:S(2)}) async-start(bf16[8,8,7168]{2,1,0:T(8,128)(2,1)} %bitcast.64), calls=%async_computation.3 | async-start | bytes 1835008 | tf_op jit(solution)/shard_map/all_to_all | solution.py:47

commit v2 on v1

--- a/solution.py
+++ b/solution.py
@@ -21,7 +21,7 @@
 TABLE = 128
 SLOT_ROWS = 24
 EDGES = (0, 2560, 7168)
-OUT_EDGES = (0, 2816, 5632, 7168)
+OUT_EDGES = (0, 2560, 5120, 7168)
 
 
 def code_of(dev):

time: 147 us -> 147 us (level)
  transfers between devices with their start and end apart: 8 -> 8, of which waited for: 7 -> 6; matrix products, arithmetic and copies ran while one was open for 11% -> 11% of each run, Pallas kernels for 0% -> 0%
where the time goes in v2:
time: 147 us
  waiting for transfers between devices  51.2 us (35%)
  blocking collectives  42.4 us (29%)
  matrix products  17.3 us (12%)
  starting transfers between devices  17.2 us (12%)
  local copies, waits for them, and re-layouts  6.31 us (4%)
  Pallas kernels  6.13 us (4%)
  other arithmetic  4.72 us (3%)
  between operations  1.75 us (1%)
    all_to_all x3, waiting for transfers between devices, cube_exchange(): lax.all_to_all(rows, AXES, 0, 0, tiled=True, axis_index_groups=groups)  48.3 us
    all_to_all x1, blocking collectives, cube_exchange(): lax.all_to_all(rows, AXES, 0, 0, tiled=True, axis_index_groups=groups)  42.4 us
    all_to_all x3, starting transfers between devices, cube_exchange(): lax.all_to_all(rows, AXES, 0, 0, tiled=True, axis_index_groups=groups)  14.1 us
    pallas_call x1, Pallas kernels, spread(): pl.pallas_call(spread_kernel, grid=(2,), in_specs=[pl.BlockSpec((tokens,...  4.03 us
    dynamic_update_slice x7, local copies, waits for them, and re-layouts, local(): lax.dynamic_update_slice(back, rows.reshape(CUBE, 1, SLOT_ROWS, -1), (0,...  3.97 us
    dot_general x3, matrix products, local(): jnp.dot(inner_act, w_down[:, OUT_EDGES[i]:OUT_EDGES[i + 1]], preferred_el...  3.49 us
    dot_general x1, matrix products, attend(): jnp.einsum('rhl,rlc->rhc', weights, cache[:, :, :LATENT], preferred_eleme...  3.4 us
    dot_general x2, matrix products, local(): up = jnp.dot(work, w_gate_up[1, cols], preferred_element_type=jnp.float32)  3.15 us
  transfers between devices with their start and end apart: 8, of which 6 were waited for; matrix products, arithmetic and copies ran while one was open for 11% of the time, Pallas kernels for 0%

profile of v2, /device:TPU:1, one launch (start us, length us, event | category | flops | bytes accessed | tf_op | source)
XLA Modules:
  0.0 147.0 jit_solution(1596707160602650485)
XLA Ops:
  0.6 2.1 %shard_map.122 = bf16[64,7296]{1,0:T(8,128)(2,1)} custom-call(bf16[8,7168]{1,0:T(8,128)(2,1)} %hidden_ref.1, s32[8,8]{1,0:T(8,128)} %routes_ref.1, s32[8,8]{1,0:T(8,128)} %codes_ref.1), custom_call_target="tpu_custom_call" | custom-call | tf_op jit(solution)/shard_map/pallas_call | solution.py:90
  2.7 5.9 %all-to-all-start = ((bf16[8,8,7296]{2,1,0:T(8,128)(2,1)}), bf16[8,8,7296]{2,1,0:T(8,128)(2,1)S(1)}, u32[]{:S(2)}, u32[]{:S(2)}) async-start(bf16[8,8,7296]{2,1,0:T(8,128)(2,1)} %bitcast.61), calls=%async_computation | async-start | bytes 1867776 | tf_op jit(solution)/shard_map/all_to_all | solution.py:47
  8.7 0.7 broadcast_select_fusion
  9.4 0.6 slice.70
  10.6 0.7 add_bitcast_fusion.1
  12.1 0.8 select_reduce_fusion
  13.0 5.6 %all-to-all-done = bf16[8,8,7296]{2,1,0:T(8,128)(2,1)S(1)} async-done(((bf16[8,8,7296]{2,1,0:T(8,128)(2,1)}), bf16[8,8,7296]{2,1,0:T(8,128)(2,1)S(1)}, u32[]{:S(2)}, u32[]{:S(2)}) %all-to-all-start) | async-done | bytes 933920 | tf_op jit(solution)/shard_map/all_to_all | solution.py:47
  18.6 0.2 fusion.28
  18.8 0.1 copy.25
  19.0 1.7 %convolution_convert_fusion = bf16[384,7168]{1,0:T(8,128)(2,1)S(1)} fusion(bf16[64,7296]{1,0:T(8,128)(2,1)S(1)} %bitcast.63, f32[384,64]{0,1:T(8,128)S(1)} %copy.25, s32[384]{0:T(512)S(1)} %iota.91, s32[384]{0:T(512)S(1)} %iota.88, s32[64]{0:T(128)S(1)} %get-tuple-element.40, s32[64]{0:T(128)S(1)} %get-tuple-element.41, s32[384]{0:T(512)S(1)} %iota.76, ...), kind=kOutput, calls=%fused_computation.1 | convolution fusion | flops 355270656 | bytes 6531584 | tf_op jit(solution)/shard_map/dot_general | solution.py:160
  20.7 42.4 %all_to_all.41 = bf16[8,48,7168]{2,1,0:T(8,128)(2,1)S(1)} all-to-all(bf16[8,48,7168]{2,1,0:T(8,128)(2,1)S(1)} %bitcast.54), channel_id=1, replica_groups={{0,12,16,28,4,8,20,24},{1,13,17,29,5,9,21,25},{3,15,19,31,7,11,23,27},{..., dimensions={0} | all-to-all | bytes 11010048 | tf_op jit(solution)/shard_map/all_to_all | solution.py:47
  63.1 0.1 fusion.37
  63.3 1.9 %collective-permute-start.1 = (bf16[192,2560]{1,0:T(8,128)(2,1)S(1)}, bf16[192,2560]{1,0:T(8,128)(2,1)S(1)}, u32[]{:S(2)}, u32[]{:S(2)}) collective-permute-start(bf16[192,2560]{1,0:T(8,128)(2,1)S(1)} %bitcast.71), channel_id=1, source_target_pairs={{0,64},{64,0},{1,65},{65,1},{2,66},{66,2},{3,67},{67,3},{4,68},{68... | collective-permute-start | bytes 2949128 | tf_op jit(solution)/shard_map/ppermute | solution.py:51
  65.2 0.2 fusion.38
  65.4 0.1 collective-permute-start
  65.5 1.9 %collective-permute-done.1 = bf16[192,2560]{1,0:T(8,128)(2,1)S(1)} collective-permute-done((bf16[192,2560]{1,0:T(8,128)(2,1)S(1)}, bf16[192,2560]{1,0:T(8,128)(2,1)S(1)}, u32[]{:S(2)}, u32[]{:S(2)}) %collective-permute-start.1) | collective-permute-done | bytes 983072 | tf_op jit(solution)/shard_map/ppermute | solution.py:51
  67.4 1.2 fusion.9
  68.6 1.2 fusion.7
  69.7 0.2 collective-permute-done
  69.9 0.2 pad_maximum_fusion
  70.1 2.0 %fusion.1 = f32[384,512]{1,0:T(8,128)S(1)} fusion(bf16[384,4608]{1,0:T(8,128)(2,1)S(1)} %pad_maximum_fusion, bf16[2,7168,512]{2,1,0:T(8,128)(2,1)S(1)} %bitcast.76), kind=kOutput, calls=%fused_computation.2 | convolution fusion | flops 1811939328 | bytes 9043968 | tf_op jit(solution)/shard_map/dot_general | solution.py:173
  72.1 2.0 %fusion.3 = f32[384,512]{1,0:T(8,128)S(1)} fusion(bf16[384,4608]{1,0:T(8,128)(2,1)S(1)} %pad_maximum_fusion, bf16[2,7168,512]{2,1,0:T(8,128)(2,1)S(1)} %bitcast.76), kind=kOutput, calls=%fused_computation.4 | convolution fusion | flops 1811939328 | bytes 9043968 | tf_op jit(solution)/shard_map/dot_general | solution.py:172
  74.1 0.4 multiply_convert_fusion
  74.6 1.2 convolution_convert_fusion.2
  75.8 0.1 fusion.40
  76.0 0.5 collective-permute-start.2
  76.4 1.2 convolution_convert_fusion.1
  77.7 0.1 fusion.39
  77.8 0.2 collective-permute-start.3
  78.0 1.0 convolution_convert_fusion.3
  79.0 0.1 fusion.41
  79.2 0.5 collective-permute-start.4
  79.6 0.6 dynamic_update_slice.18
  80.3 0.1 constant_dynamic-update-slice_fusion.4
  80.4 0.1 constant_dynamic-update-slice_fusion.3
  80.7 0.9 collective-permute-done.4
  81.6 2.9 %copy.27 = bf16[8,2,24,7168]{3,2,1,0:T(8,128)(2,1)} copy(bf16[8,2,24,7168]{3,2,0,1:T(8,128)(2,1)S(1)} %constant_dynamic-update-slice_fusion) | data formatting | bytes 11010048 | tf_op jit(solution)/shard_map/dynamic_update_slice | solution.py:186
  84.6 4.7 %all-to-all-start.2 = ((bf16[8,48,7168]{2,1,0:T(8,128)(2,1)}), bf16[8,48,7168]{2,1,0:T(8,128)(2,1)}, u32[]{:S(2)}, u32[]{:S(2)}) async-start(bf16[8,48,7168]{2,1,0:T(8,128)(2,1)} %bitcast.55), calls=%async_computation.2 | async-start | bytes 11010048 | tf_op jit(solution)/shard_map/all_to_all | solution.py:47
  89.3 0.1 copy.26
  89.4 0.7 fusion.27.factors_ref
  90.1 38.7 %all-to-all-done.2 = bf16[8,48,7168]{2,1,0:T(8,128)(2,1)} async-done(((bf16[8,48,7168]{2,1,0:T(8,128)(2,1)}), bf16[8,48,7168]{2,1,0:T(8,128)(2,1)}, u32[]{:S(2)}, u32[]{:S(2)}) %all-to-all-start.2) | async-done | bytes 5505056 | tf_op jit(solution)/shard_map/all_to_all | solution.py:47
  128.8 4.0 %shard_map.123 = bf16[64,7168]{1,0:T(8,128)(2,1)} custom-call(bf16[64,384]{1,0:T(8,128)(2,1)} %fusion.27.factors_ref, bf16[384,7168]{1,0:T(8,128)(2,1)} %bitcast.28.rows_ref), custom_call_target="tpu_custom_call" | custom-call | tf_op jit(solution)/shard_map/pallas_call | solution.py:138
  132.8 3.6 %all-to-all-start.3 = ((bf16[8,8,7168]{2,1,0:T(8,128)(2,1)}), bf16[8,8,7168]{2,1,0:T(8,128)(2,1)S(1)}, u32[]{:S(2)}, u32[]{:S(2)}) async-start(bf16[8,8,7168]{2,1,0:T(8,128)(2,1)} %bitcast.64), calls=%async_computation.3 | async-start | bytes 1835008 | tf_op jit(solution)/shard_map/all_to_all | solution.py:47
  136.4 2.2 %fusion.23 = f32[8,64,256]{2,1,0:T(8,128)S(1)} fusion(bf16[8,64,576]{2,1,0:T(8,128)(2,1)S(1)} %copy-done, bf16[8,256,576]{1,2,0:T(8,128)(2,1)} %param.12, s32[8]{0:T(128)S(1)} %copy-done.1), kind=kOutput, calls=%fused_computation.28 | convolution fusion | flops 151388160 | bytes 3473440 | tf_op jit(solution)/shard_map/rhc,rlc->rhl/dot_general | solution.py:56
  138.6 0.2 fusion.42
  138.9 3.4 %fusion.18 = bf16[8,64,512]{2,1,0:T(8,128)(2,1)} fusion(bf16[8,256,576]{1,2,0:T(8,128)(2,1)} %param.12, f32[8,64]{1,0:T(8,128)S(1)} %fusion.42, f32[8,64,256]{2,1,0:T(8,128)S(1)} %fusion.23), kind=kOutput, calls=%fused_computation.24 | convolution fusion | flops 134873856 | bytes 3674112 | tf_op jit(solution)/shard_map/rhl,rlc->rhc/dot_general | solution.py:63
  142.2 4.0 %all-to-all-done.3 = bf16[8,8,7168]{2,1,0:T(8,128)(2,1)S(1)} async-done(((bf16[8,8,7168]{2,1,0:T(8,128)(2,1)}), bf16[8,8,7168]{2,1,0:T(8,128)(2,1)S(1)}, u32[]{:S(2)}, u32[]{:S(2)}) %all-to-all-start.3) | async-done | bytes 917536 | tf_op jit(solution)/shard_map/all_to_all | solution.py:47
  146.2 0.8 reduce_sum.32
  (52 shorter events, 1.2 us)
Async XLA Ops:
  0.6 135.7 %copy-start = (bf16[8,64,576]{2,1,0:T(8,128)(2,1)S(1)}, bf16[8,64,576]{2,1,0:T(8,128)(2,1)}, u32[]{:S(2)}) copy-start(bf16[8,64,576]{2,1,0:T(8,128)(2,1)} %param.11) | copy-start | bytes 1769476
  2.7 15.9 %all-to-all-start = ((bf16[8,8,7296]{2,1,0:T(8,128)(2,1)}), bf16[8,8,7296]{2,1,0:T(8,128)(2,1)S(1)}, u32[]{:S(2)}, u32[]{:S(2)}) async-start(bf16[8,8,7296]{2,1,0:T(8,128)(2,1)} %bitcast.61), calls=%async_computation | async-start | bytes 1867776 | tf_op jit(solution)/shard_map/all_to_all | solution.py:47
  19.0 48.4 %slice-start = ((s8[14680064]{0:T(1024)(128)(4,1)}), s8[4194304]{0:T(1024)(128)(4,1)S(1)}, s32[]{:S(2)}) async-start(s8[14680064]{0:T(1024)(128)(4,1)} %bitcast.75), calls=%async_computation.4 | async-start | bytes 8388608
  19.0 48.4 %slice-start.1 = ((s8[14680064]{0:T(1024)(128)(4,1)}), s8[4194304]{0:T(1024)(128)(4,1)S(1)}, s32[]{:S(2)}) async-start(s8[14680064]{0:T(1024)(128)(4,1)} %bitcast.75), calls=%async_computation.5 | async-start | bytes 8388608
  20.7 46.7 %slice-start.2 = ((s8[14680064]{0:T(1024)(128)(4,1)}), s8[4194304]{0:T(1024)(128)(4,1)S(1)}, s32[]{:S(2)}) async-start(s8[14680064]{0:T(1024)(128)(4,1)} %bitcast.75), calls=%async_computation.6 | async-start | bytes 8388608
  63.1 4.2 %slice-start.3 = ((s8[14680064]{0:T(1024)(128)(4,1)}), s8[2097152]{0:T(1024)(128)(4,1)S(1)}, s32[]{:S(2)}) async-start(s8[14680064]{0:T(1024)(128)(4,1)} %bitcast.75), calls=%async_computation.7 | async-start | bytes 4194304
  63.3 4.1 %collective-permute-start.1 = (bf16[192,2560]{1,0:T(8,128)(2,1)S(1)}, bf16[192,2560]{1,0:T(8,128)(2,1)S(1)}, u32[]{:S(2)}, u32[]{:S(2)}) collective-permute-start(bf16[192,2560]{1,0:T(8,128)(2,1)S(1)} %bitcast.71), channel_id=1, source_target_pairs={{0,64},{64,0},{1,65},{65,1},{2,66},{66,2},{3,67},{67,3},{4,68},{68... | collective-permute-start | bytes 2949128 | tf_op jit(solution)/shard_map/ppermute | solution.py:51
  65.4 4.5 %collective-permute-start = (bf16[192,4608]{1,0:T(8,128)(2,1)S(1)}, bf16[192,4608]{1,0:T(8,128)(2,1)S(1)}, u32[]{:S(2)}, u32[]{:S(2)}) collective-permute-start(bf16[192,4608]{1,0:T(8,128)(2,1)S(1)} %bitcast.66), channel_id=1, source_target_pairs={{0,64},{64,0},{1,65},{65,1},{2,66},{66,2},{3,67},{67,3},{4,68},{68... | collective-permute-start | bytes 5308424 | tf_op jit(solution)/shard_map/ppermute | solution.py:51
  70.1 4.4 %slice-start.4 = ((s8[7340032]{0:T(1024)(128)(4,1)}), s8[4194304]{0:T(1024)(128)(4,1)S(1)}, s32[]{:S(2)}) async-start(s8[7340032]{0:T(1024)(128)(4,1)} %bitcast.77), calls=%async_computation.8 | async-start | bytes 8388608
  72.1 2.4 %slice-start.5 = ((s8[7340032]{0:T(1024)(128)(4,1)}), s8[3145728]{0:T(1024)(128)(4,1)S(1)}, s32[]{:S(2)}) async-start(s8[7340032]{0:T(1024)(128)(4,1)} %bitcast.77), calls=%async_computation.9 | async-start | bytes 6291456
  76.0 4.3 %collective-permute-start.2 = (bf16[192,2560]{1,0:T(8,128)(2,1)S(1)}, bf16[192,2560]{1,0:T(8,128)(2,1)S(1)}, u32[]{:S(2)}, u32[]{:S(2)}) collective-permute-start(bf16[192,2560]{1,0:T(8,128)(2,1)S(1)} %get-tuple-element.19), channel_id=1, source_target_pairs={{0,64},{64,0},{1,65},{65,1},{2,66},{66,2},{3,67},{67,3},{4,68},{68... | collective-permute-start | bytes 2949128 | tf_op jit(solution)/shard_map/ppermute | solution.py:51
  77.8 2.7 %collective-permute-start.3 = (bf16[192,2560]{1,0:T(8,128)(2,1)S(1)}, bf16[192,2560]{1,0:T(8,128)(2,1)S(1)}, u32[]{:S(2)}, u32[]{:S(2)}) collective-permute-start(bf16[192,2560]{1,0:T(8,128)(2,1)S(1)} %get-tuple-element.23), channel_id=1, source_target_pairs={{0,64},{64,0},{1,65},{65,1},{2,66},{66,2},{3,67},{67,3},{4,68},{68... | collective-permute-start | bytes 2949128 | tf_op jit(solution)/shard_map/ppermute | solution.py:51
  79.2 2.4 %collective-permute-start.4 = (bf16[192,2048]{1,0:T(8,128)(2,1)S(1)}, bf16[192,2048]{1,0:T(8,128)(2,1)S(1)}, u32[]{:S(2)}, u32[]{:S(2)}) collective-permute-start(bf16[192,2048]{1,0:T(8,128)(2,1)S(1)} %get-tuple-element.36), channel_id=1, source_target_pairs={{0,64},{64,0},{1,65},{65,1},{2,66},{66,2},{3,67},{67,3},{4,68},{68... | collective-permute-start | bytes 2359304 | tf_op jit(solution)/shard_map/ppermute | solution.py:51
  84.6 44.2 %all-to-all-start.2 = ((bf16[8,48,7168]{2,1,0:T(8,128)(2,1)}), bf16[8,48,7168]{2,1,0:T(8,128)(2,1)}, u32[]{:S(2)}, u32[]{:S(2)}) async-start(bf16[8,48,7168]{2,1,0:T(8,128)(2,1)} %bitcast.55), calls=%async_computation.2 | async-start | bytes 11010048 | tf_op jit(solution)/shard_map/all_to_all | solution.py:47
  128.8 7.6 %copy-start.1 = (s32[8]{0:T(128)S(1)}, s32[8]{0:T(128)}, u32[]{:S(2)}) copy-start(s32[8]{0:T(128)} %param.13) | copy-start | bytes 100
  132.8 13.4 %all-to-all-start.3 = ((bf16[8,8,7168]{2,1,0:T(8,128)(2,1)}), bf16[8,8,7168]{2,1,0:T(8,128)(2,1)S(1)}, u32[]{:S(2)}, u32[]{:S(2)}) async-start(bf16[8,8,7168]{2,1,0:T(8,128)(2,1)} %bitcast.64), calls=%async_computation.3 | async-start | bytes 1835008 | tf_op jit(solution)/shard_map/all_to_all | solution.py:47
